TPU v7x, 256 devices: a whole 4x4x8 slice. The times are simulated.
256 devices in a mesh: code: 128 (over y, z, x_lo, core), dp: 2 (over x_hi).
Axes of the slice: x: 4 (x_hi: 2, x_lo: 2; x = x_hi * 2 + x_lo), y: 4, z: 8, core: 2. Of those that a mesh axis runs over, the one named last changes fastest.
Arguments:
- latents: bfloat16 [2, 4096, 256], P('dp', 'code'), may hold values from -24 to 24
- codebook: bfloat16 [131072, 256], P('code'), may hold values from -0.7 to 0.7
- cotangent: bfloat16 [2, 4096, 256], P('dp', 'code'), may hold values from -6 to 6
Outputs:
- quantized: bfloat16 [2, 4096, 256], P('dp', 'code')
- code_grad: float32 [131072, 256], P('code')
All inputs are finite; a program needn't handle non-finite values.
Results may differ from a plain program's by a relative error of at most 0.0095.
Values may be sent and summed in bfloat16 or wider, within the bound.
A program may use at most 128 MiB of HBM per device.

v0:
```python
import jax
import jax.numpy as jnp
from jax import lax
from jax.sharding import PartitionSpec as P


def shard_grad(rows_lat, rows_cot, block, top, total, inner):
    by_feature = (((1,), (1,)), ((), ()))
    by_token = (((0,), (0,)), ((), ()))
    block_f32 = block.astype(jnp.float32)
    half = 0.5 * jnp.sum(block_f32 * block_f32, axis=1)
    scores = (
        lax.dot_general(rows_lat, block, by_feature, preferred_element_type=jnp.float32)
        - half[None, :]
    )
    prob = jnp.exp(scores - top[:, None]) / total[:, None]
    align = lax.dot_general(rows_cot, block, by_feature, preferred_element_type=jnp.float32)
    slope = prob * (align - inner[:, None])
    first = lax.dot_general(
        prob.astype(jnp.bfloat16), rows_cot, by_token, preferred_element_type=jnp.float32
    )
    second = lax.dot_general(
        slope.astype(jnp.bfloat16), rows_lat, by_token, preferred_element_type=jnp.float32
    )
    return first + second - jnp.sum(slope, axis=0)[:, None] * block_f32


def body(latents, codebook, cotangent):
    own_lat = latents[0]
    own_cot = cotangent[0]
    all_lat, all_cot = (
        lax.all_gather(own_lat, "code", axis=0, tiled=True),
        lax.all_gather(own_cot, "code", axis=0, tiled=True),
    )
    code_f32 = codebook.astype(jnp.float32)
    half_norm = 0.5 * jnp.sum(code_f32 * code_f32, axis=1)
    by_feature = (((1,), (1,)), ((), ()))
    logits = (
        lax.dot_general(all_lat, codebook, by_feature, preferred_element_type=jnp.float32)
        - half_norm[None, :]
    )
    top = lax.pmax(jnp.max(logits, axis=1), "code")
    expo = jnp.exp(logits - top[:, None])
    total = lax.psum(jnp.sum(expo, axis=1), "code")
    weights = expo.astype(jnp.bfloat16)
    own_rows = own_lat.shape[0]
    own_start = lax.axis_index("code") * own_rows
    own_mixed = lax.psum_scatter(
        jnp.dot(weights, codebook, preferred_element_type=jnp.float32),
        "code",
        scatter_dimension=0,
        tiled=True,
    )
    own_total = lax.dynamic_slice_in_dim(total, own_start, own_rows, 0)
    own_quant = own_mixed / own_total[:, None]
    own_inner = jnp.sum(own_cot.astype(jnp.float32) * own_quant, axis=1)
    inner = lax.all_gather(own_inner, "code", axis=0, tiled=True)
    scale = (
        codebook.shape[0] * lax.axis_size("code") * 1.0 / (lax.axis_size("dp") * all_lat.shape[0])
    )
    local_grad = shard_grad(all_lat, all_cot, codebook, top, total, inner)
    summed = lax.psum(local_grad.astype(jnp.bfloat16), "dp").astype(jnp.float32)
    return (own_quant.astype(jnp.bfloat16)[None], summed * scale)


def solution(mesh):
    in_specs = (P("dp", "code", None), P("code", None), P("dp", "code", None))
    out_specs = (P("dp", "code", None), P("code", None))
    return jax.shard_map(body, mesh=mesh, in_specs=in_specs, out_specs=out_specs, check_vma=False)
```

profile of v0, /device:TPU:6, one launch (start us, length us, event | category | flops | bytes accessed | tf_op | source)
XLA Modules:
  0.0 1973.0 jit_solution(12623658902980179050)
XLA Ops:
  7.2 0.0 all-gather.5.cloned.1.call-start
  7.2 0.7 all-gather.5.cloned.1.call-update
  7.9 0.0 reduce-scatter.2.cloned.1.call-start
  8.0 1.3 fusion.31
  9.2 216.6 %all-gather.5.cloned.1.call-done = bf16[1,4096,256]{2,1,0:T(8,128)(2,1)} async-done(((bf16[1,32,256]{2,1,0:T(8,128)(2,1)}), bf16[1,4096,256]{2,1,0:T(8,128)(2,1)}) %all-gather.5.cloned.1.call-update) | async-done | bytes 2097168 | tf_op jit(solution)/shard_map/all_gather | solution.py:32
  225.8 9.8 subtract_reduce_fusion
  235.6 544.2 %pmax.7 = f32[4096]{0:T(1024)S(1)} all-reduce(f32[4096]{0:T(1024)S(1)} %get-tuple-element.4), channel_id=1, replica_groups=mesh['code'=128,'dp'=2] {'code'}, use_global_device_ids=true, to_apply=%region_2.0 | all-reduce | flops 4096 | bytes 32768 | tf_op jit(solution)/shard_map/pmax | solution.py:42
  779.8 11.1 fusion.3
  791.0 0.0 all-gather.7.cloned.1.call-start
  791.0 0.7 all-gather.7.cloned.1.call-update
  791.7 0.0 all-reduce.3.cloned.1.call-start
  791.8 0.6 dynamic-slice
  793.0 9.3 fusion.1
  802.3 548.8 %psum.14 = f32[4096]{0:T(1024)S(1)} all-reduce(f32[4096]{0:T(1024)S(1)} %fusion.1), channel_id=1, replica_groups=mesh['code'=128,'dp'=2] {'code'}, use_global_device_ids=true, to_apply=%region_5.0 | all-reduce | flops 4096 | bytes 32768 | tf_op jit(solution)/shard_map/psum | solution.py:44
  1351.0 0.1 dynamic_slice.3
  1351.1 2.3 reduce-scatter.2.cloned.1.call-done
  1353.4 1.5 fusion.32
  1354.9 0.3 dynamic-update-slice
  1355.2 548.7 %all-reduce = f32[4096]{0:T(1024)S(1)} all-reduce(f32[4096]{0:T(1024)S(1)} %dynamic-update-slice), channel_id=1, replica_groups=mesh['code'=128,'dp'=2] {'code'}, use_global_device_ids=true, to_apply=%add | all-reduce | flops 4096 | bytes 32768
  1904.0 9.9 fusion.34
  1913.9 2.4 fusion.5
  1916.3 8.3 fusion.26
  1924.6 39.7 %all-reduce.3.cloned.1.call-done = bf16[1024,256]{1,0:T(8,128)(2,1)} async-done(((bf16[1024,256]{1,0:T(8,128)(2,1)}), bf16[1024,256]{1,0:T(8,128)(2,1)}) %all-reduce.3.cloned.1.call-update) | async-done | bytes 524304 | tf_op jit(solution)/shard_map/psum | solution.py:62
  1964.4 2.1 convert_multiply_fusion.2
  (15 shorter events, 0.1 us)
Async XLA Ops:
  7.2 772.6 %copy-start.1 = (bf16[1024,256]{1,0:T(8,128)(2,1)S(1)}, bf16[1024,256]{1,0:T(8,128)(2,1)}, u32[]{:S(2)}) copy-start(bf16[1024,256]{1,0:T(8,128)(2,1)} %param.4) | copy-start | bytes 1572868
  7.2 218.6 %all-gather.5.cloned.1.call-start = ((), (), s32[]{:S(2)}) async-start(), calls=%async_computation.3 | async-start | bytes 2113536 | tf_op jit(solution)/shard_map/all_gather | solution.py:32
  7.9 1345.5 %reduce-scatter.2.cloned.1.call-start = ((), (), s32[]{:S(2)}) async-start(), calls=%async_computation.1 | async-start | bytes 4227072 | tf_op jit(solution)/shard_map/reduce_scatter | solution.py:48
  779.8 12.0 copy-start.4
  791.0 562.4 %copy-start.2 = (bf16[1,32,256]{2,1,0:T(8,128)(2,1)S(1)}, bf16[1,32,256]{2,1,0:T(8,128)(2,1)}, u32[]{:S(2)}) copy-start(bf16[1,32,256]{2,1,0:T(8,128)(2,1)} %param.5) | copy-start | bytes 49156
  791.0 1113.0 %all-gather.7.cloned.1.call-start = ((), (), s32[]{:S(2)}) async-start(), calls=%async_computation.4 | async-start | bytes 2113536 | tf_op jit(solution)/shard_map/all_gather | solution.py:33
  791.7 1172.6 %all-reduce.3.cloned.1.call-start = ((), (), s32[]{:S(2)}) async-start(), calls=%async_computation.2 | async-start | bytes 1048576 | tf_op jit(solution)/shard_map/psum | solution.py:62
  1903.9 10.0 copy-start
  1903.9 12.3 copy-start.3
Sparse Core Ops, SparseCore 0:
  9.9 215.8 all-gather.4
  791.1 562.2 reduce-scatter.1
  1355.4 212.3 all-gather.6
  1924.8 39.5 all-reduce.2
where the time goes:
time: 1980 us; the launch traced here: 1970 us
  blocking collectives  1640 us (83%)
  waiting for transfers between devices  260 us (13%)
  matrix products  41.5 us (2%)
    psum x1, blocking collectives, body(): total = lax.psum(jnp.sum(expo, axis=1), 'code')  549 us
    unnamed x1, blocking collectives  549 us
    pmax x1, blocking collectives, body(): top = lax.pmax(jnp.max(logits, axis=1), 'code')  544 us
    all_gather x1, waiting for transfers between devices, body(): lax.all_gather(own_lat, 'code', axis=0, tiled=True)  217 us
    psum x1, waiting for transfers between devices, body(): summed = lax.psum(local_grad.astype(jnp.bfloat16), 'dp').astype(jnp.float32)  39.7 us
  transfers between devices with their start and end apart: 4, of which 3 were waited for; matrix products, arithmetic and copies ran while one was open for 1% of the time, Pallas kernels for 0%

commit v1 on v0

v1 whole, which is shorter than its diff:
```python
import functools

import jax
import jax.numpy as jnp
from jax import lax
from jax.experimental import pallas as pl
from jax.experimental.pallas import tpu as pltpu
from jax.sharding import PartitionSpec as P

MESH = pl.DeviceIdType.MESH
NY, NZ, NX, NC = 4, 8, 2, 2
NB = NY * NX
NPLANE = NB * NC
BF, F32 = jnp.bfloat16, jnp.float32
CHUNK = 256
BY_LANE = (((1,), (1,)), ((), ()))


def kernel(
    scale, lat_ref, cb_ref, cot_ref, q_ref, g_ref,
    rows, expo, align, mixed, code_t, half, stats, zparts, pparts, final, gain,
    qpart, qcore, qy, qysum, qx, qxsum, qz, acc, slope_sum, gown, gin,
    ag_s, ag_r, ring_s, ring_r, sib_s, sib_r, zs_s, zs_r, pp_s, pp_r, za_s, za_r,
    qc_s, qc_r, qy_s, qy_r, qx_s, qx_r, qz_s, qz_r, dp_s, dp_r,
):
    me = lax.axis_index("code")
    rep = lax.axis_index("dp")
    c = me % NC
    x = (me // NC) % NX
    z = (me // (NC * NX)) % NZ
    y = me // (NC * NX * NZ)
    b = y * NX + x
    q = b * NC + c
    own = lat_ref.shape[0]
    tile = NB * own
    n_codes, width = cb_ref.shape
    n_chunks = n_codes // CHUNK

    def dev(y_, z_, x_, c_):
        return {"code": ((y_ * NZ + z_) * NX + x_) * NC + c_}

    def send(src, dst, s_sem, r_sem, device):
        return pltpu.make_async_remote_copy(
            src_ref=src, dst_ref=dst, send_sem=s_sem, recv_sem=r_sem,
            device_id=device, device_id_type=MESH,
        )

    def plane_dev(p_):
        b_ = p_ // NC
        return dev(b_ // NX, z, b_ % NX, p_ % NC)

    sibling = dev(y, z, x, 1 - c)
    other_dp = {"dp": 1 - rep}

    barrier = pltpu.get_barrier_semaphore()
    for d in range(1, NPLANE):
        pl.semaphore_signal(barrier, inc=1, device_id=plane_dev((q + d) % NPLANE), device_id_type=MESH)
    for d in range(1, NZ):
        pl.semaphore_signal(barrier, inc=1, device_id=dev(y, (z + d) % NZ, x, c), device_id_type=MESH)
    pl.semaphore_signal(barrier, inc=1, device_id=other_dp, device_id_type=MESH)

    own_rows = pl.ds(pl.multiple_of(b * own, own), own)
    rows[z, c, 0, own_rows, :] = lat_ref[...]
    rows[z, c, 1, own_rows, :] = cot_ref[...]

    pl.semaphore_wait(barrier, NPLANE - 1 + NZ - 1 + 1)

    def gather_copy(d):
        b_ = (b + d) % NB
        block = rows.at[z, c, :, own_rows, :]
        return send(block, block, ag_s.at[d], ag_r.at[d], dev(b_ // NX, z, b_ % NX, c))

    for d in range(1, NB):
        gather_copy(d).start()

    for k in range(n_chunks):
        part = cb_ref[k * CHUNK:(k + 1) * CHUNK, :].astype(F32)
        norm = 0.5 * jnp.sum(part * part, axis=1, keepdims=True)
        half[k * CHUNK:(k + 1) * CHUNK, :] = jnp.broadcast_to(norm, (CHUNK, tile))
        code_t[:, k * CHUNK:(k + 1) * CHUNK] = jnp.transpose(part).astype(BF)

    def gather_wait(d):
        b_ = (b + NB - d) % NB
        block = rows.at[z, c, :, pl.ds(pl.multiple_of(b_ * own, own), own), :]
        send(block, block, ag_s.at[d], ag_r.at[d], dev(y, z, x, 1 - c)).wait_recv()

    for d in range(1, NB):
        gather_wait(d)

    def zat(direction, step):
        return (z + NZ - step) % NZ if direction == 0 else (z + step) % NZ

    def ring_copy(direction, step, f):
        block = rows.at[zat(direction, step - 1), c, f]
        to = (z + 1) % NZ if direction == 0 else (z + NZ - 1) % NZ
        return send(block, block, ring_s.at[direction, step, f], ring_r.at[direction, step, f], dev(y, to, x, c))

    def ring_wait(direction, step, f):
        block = rows.at[zat(direction, step), c, f]
        send(block, block, ring_s.at[direction, step, f], ring_r.at[direction, step, f], sibling).wait_recv()

    def sib_copy(direction, step, f):
        block = rows.at[zat(direction, step), c, f]
        return send(block, block, sib_s.at[direction, step, f], sib_r.at[direction, step, f], sibling)

    def sib_wait(direction, step, f):
        block = rows.at[zat(direction, step), 1 - c, f]
        send(block, block, sib_s.at[direction, step, f], sib_r.at[direction, step, f], sibling).wait_recv()

    def scatter_copy(d):
        to = (z + d) % NZ
        return send(stats.at[to], zparts.at[z], zs_s.at[d], zs_r.at[d], dev(y, to, x, c))

    def tile_forward(zp, cp):
        lat = rows[zp, cp, 0]
        cot = rows[zp, cp, 1]
        top8 = None
        for k in range(n_chunks):
            ks = slice(k * CHUNK, (k + 1) * CHUNK)
            code = cb_ref[ks, :]
            logit = lax.dot_general(code, lat, BY_LANE, preferred_element_type=F32) - half[ks, :]
            expo[zp, cp, ks, :] = logit
            align[zp, cp, ks, :] = lax.dot_general(code, cot, BY_LANE, preferred_element_type=F32)
            part = jnp.max(logit.reshape(CHUNK // 8, 8, tile), axis=0)
            top8 = part if top8 is None else jnp.maximum(top8, part)
        top = jnp.max(top8, axis=0, keepdims=True)
        total8 = jnp.zeros((8, tile), F32)
        inner8 = jnp.zeros((8, tile), F32)
        mix = jnp.zeros((width, tile), F32)
        for k in range(n_chunks):
            ks = slice(k * CHUNK, (k + 1) * CHUNK)
            e = jnp.exp(expo[zp, cp, ks, :] - top)
            expo[zp, cp, ks, :] = e
            total8 += jnp.sum(e.reshape(CHUNK // 8, 8, tile), axis=0)
            inner8 += jnp.sum((e * align[zp, cp, ks, :]).reshape(CHUNK // 8, 8, tile), axis=0)
            mix += jnp.dot(code_t[:, ks], e.astype(BF), preferred_element_type=F32)
        mixed[zp, cp] = mix
        total = jnp.sum(total8, axis=0, keepdims=True)
        inner = jnp.sum(inner8, axis=0, keepdims=True)
        stats[zp, cp] = jnp.concatenate([top, total, inner, inner], axis=0)

    for f in range(2):
        for direction in range(2):
            ring_copy(direction, 1, f).start()
        sib_copy(0, 0, f).start()
    last = NZ // 2

    @pl.loop(0, 2)
    def _(j):
        @pl.when(j == 1)
        def _():
            sib_wait(0, 0, 0)
            sib_wait(0, 0, 1)
        tile_forward(z, (c + j) % 2)

    zparts[z] = stats[z]

    @pl.loop(1, last)
    def _(s):
        for f in range(2):
            for direction in range(2):
                ring_wait(direction, s, f)
                if direction == f:
                    ring_copy(direction, s + 1, f).start()
                else:
                    @pl.when(s + 1 < last)
                    def _():
                        ring_copy(direction, s + 1, f).start()
                sib_copy(direction, s, f).start()

        @pl.loop(0, 4)
        def _(j):
            @pl.when(j == 2)
            def _():
                for f in range(2):
                    for direction in range(2):
                        sib_wait(direction, s, f)
            zp = jnp.where(j % 2 == 0, (z + NZ - s) % NZ, (z + s) % NZ)
            tile_forward(zp, (c + j // 2) % 2)

        scatter_copy(NZ - s).start()
        scatter_copy(s).start()

    ring_wait(0, last, 0)
    sib_copy(0, last, 0).start()
    ring_wait(1, last, 1)
    sib_copy(1, last, 1).start()

    @pl.loop(0, 2)
    def _(j):
        @pl.when(j == 1)
        def _():
            sib_wait(0, last, 0)
            sib_wait(1, last, 1)
        tile_forward((z + last) % NZ, (c + j) % 2)

    scatter_copy(last).start()

    def combine(parts, n, cp):
        top = parts[0, cp, 0:1, :]
        for j in range(1, n):
            top = jnp.maximum(top, parts[j, cp, 0:1, :])
        total = jnp.zeros_like(top)
        inner = jnp.zeros_like(top)
        for j in range(n):
            w = jnp.exp(parts[j, cp, 0:1, :] - top)
            total += w * parts[j, cp, 1:2, :]
            inner += w * parts[j, cp, 2:3, :]
        return top, total, inner

    for d in range(1, NZ):
        part = zparts.at[(z + NZ - d) % NZ]
        send(part, part, zs_s.at[d], zs_r.at[d], sibling).wait_recv()
    for cp in range(2):
        top, total, inner = combine(zparts, NZ, cp)
        pparts[q, cp] = jnp.concatenate([top, total, inner, inner], axis=0)

    def plane_copy(d):
        return send(pparts.at[q], pparts.at[q], pp_s.at[d], pp_r.at[d], plane_dev((q + d) % NPLANE))

    for d in range(1, NPLANE):
        plane_copy(d).start()
    for d in range(1, NPLANE):
        part = pparts.at[(q + NPLANE - d) % NPLANE]
        send(part, part, pp_s.at[d], pp_r.at[d], sibling).wait_recv()
    for cp in range(2):
        top, total, inner = combine(pparts, NPLANE, cp)
        inverse = 1.0 / total
        final[z, cp] = jnp.concatenate([top, inverse, inner * inverse, inner], axis=0)

    def final_copy(d):
        return send(final.at[z], final.at[z], za_s.at[d], za_r.at[d], dev(y, (z + d) % NZ, x, c))

    for d in range(1, NZ):
        final_copy(d).start()
    for d in range(1, NZ):
        part = final.at[(z + NZ - d) % NZ]
        send(part, part, za_s.at[d], za_r.at[d], sibling).wait_recv()

    def quant_tile(zp, cp):
        share = jnp.exp(stats[zp, cp, 0:1, :] - final[zp, cp, 0:1, :]) * final[zp, cp, 1:2, :]
        gain[zp, cp] = jnp.concatenate([share, final[zp, cp, 2:3, :], share, share], axis=0)
        qpart[cp, zp] = jnp.transpose(mixed[zp, cp] * share).astype(BF)

    @pl.loop(0, NZ)
    def _(zp):
        quant_tile(zp, 1 - c)

    core_copy = send(qpart.at[1 - c], qcore, qc_s.at[0], qc_r.at[0], sibling)
    core_copy.start()

    @pl.loop(0, NZ)
    def _(zp):
        quant_tile(zp, c)

    def dp_copy(k):
        return send(gown.at[k], gin.at[k], dp_s.at[k], dp_r.at[k], other_dp)

    def grad_chunk(k):
        ks = pl.ds(pl.multiple_of(k * CHUNK, CHUNK), CHUNK)
        acc[...] = jnp.zeros_like(acc)
        slope_sum[...] = jnp.zeros_like(slope_sum)

        @pl.loop(0, NZ)
        def _(zp):
            out = acc[...]
            slopes = slope_sum[...]
            for cp in range(2):
                prob = expo[zp, cp, ks, :] * gain[zp, cp, 0:1, :]
                slope = prob * (align[zp, cp, ks, :] - gain[zp, cp, 1:2, :])
                out += jnp.dot(prob.astype(BF), rows[zp, cp, 1], preferred_element_type=F32)
                out += jnp.dot(slope.astype(BF), rows[zp, cp, 0], preferred_element_type=F32)
                slopes += slope
            acc[...] = out
            slope_sum[...] = slopes

        moved = jnp.sum(slope_sum[...], axis=1, keepdims=True) * cb_ref[ks, :].astype(F32)
        gown[k] = (acc[...] - moved).astype(BF)
        dp_copy(k).start()

    @pl.loop(0, 1)
    def _(k):
        grad_chunk(k)

    core_copy.wait()

    @pl.loop(0, NZ)
    def _(zp):
        qpart[c, zp] = (qpart[c, zp].astype(F32) + qcore[zp].astype(F32)).astype(BF)

    pair = NX * own

    def y_copy(d):
        to = (y + d) % NY
        part = qpart.at[c, :, pl.ds(pl.multiple_of(to * pair, pair), pair), :]
        return send(part, qy.at[d - 1], qy_s.at[d], qy_r.at[d], dev(to, z, x, c))

    for d in range(1, NY):
        y_copy(d).start()

    @pl.loop(1, n_chunks)
    def _(k):
        grad_chunk(k)

    for d in range(1, NY):
        y_copy(d).wait_recv()
    mine = pl.ds(pl.multiple_of(y * pair, pair), pair)
    total = qpart[c, :, mine, :].astype(F32)
    for d in range(NY - 1):
        total += qy[d].astype(F32)
    qysum[...] = total.astype(BF)
    x_copy = send(qysum.at[:, pl.ds(pl.multiple_of((1 - x) * own, own), own), :], qx, qx_s.at[0], qx_r.at[0], dev(y, z, 1 - x, c))
    x_copy.start()
    x_copy.wait_recv()
    mine = pl.ds(pl.multiple_of(x * own, own), own)
    qxsum[...] = (qysum[:, mine, :].astype(F32) + qx[...].astype(F32)).astype(BF)

    def z_copy(d):
        to = (z + d) % NZ
        return send(qxsum.at[to], qz.at[d - 1], qz_s.at[d], qz_r.at[d], dev(y, to, x, c))

    for d in range(1, NZ):
        z_copy(d).start()
    for d in range(1, NZ):
        z_copy(d).wait_recv()
    quant = qxsum[z].astype(F32)
    for d in range(NZ - 1):
        quant += qz[d].astype(F32)
    q_ref[...] = quant.astype(BF)

    @pl.loop(0, n_chunks)
    def _(k):
        dp_copy(k).wait_recv()
        ks = pl.ds(pl.multiple_of(k * CHUNK, CHUNK), CHUNK)
        g_ref[ks, :] = (gown[k].astype(F32) + gin[k].astype(F32)) * scale

    for d in range(1, NB):
        gather_copy(d).wait_send()
    for f in range(2):
        sib_copy(0, 0, f).wait_send()
        for direction in range(2):
            @pl.loop(1, last)
            def _(s):
                ring_copy(direction, s, f).wait_send()
                sib_copy(direction, s, f).wait_send()
        ring_copy(f, last, f).wait_send()
        sib_copy(f, last, f).wait_send()
    for d in range(1, NZ):
        scatter_copy(d).wait_send()
        final_copy(d).wait_send()
        z_copy(d).wait_send()
    for d in range(1, NPLANE):
        plane_copy(d).wait_send()
    for d in range(1, NY):
        y_copy(d).wait_send()
    x_copy.wait_send()

    @pl.loop(0, n_chunks)
    def _(k):
        dp_copy(k).wait_send()


def body(latents, codebook, cotangent):
    own, width = latents.shape[1:]
    n_codes = codebook.shape[0]
    tile = NB * own
    n_chunks = n_codes // CHUNK
    n_tokens = own * lax.axis_size("code")
    scale = n_codes * lax.axis_size("code") * 1.0 / (lax.axis_size("dp") * n_tokens)
    vmem = pl.BlockSpec(memory_space=pltpu.VMEM)
    dma = pltpu.SemaphoreType.DMA
    half_ring = NZ // 2 + 1
    quantized, grad = pl.pallas_call(
        functools.partial(kernel, scale),
        out_shape=(
            jax.ShapeDtypeStruct((own, width), BF),
            jax.ShapeDtypeStruct((n_codes, width), F32),
        ),
        in_specs=[vmem] * 3,
        out_specs=(vmem, vmem),
        scratch_shapes=[
            pltpu.VMEM((NZ, NC, 2, tile, width), BF),
            pltpu.VMEM((NZ, NC, n_codes, tile), F32),
            pltpu.VMEM((NZ, NC, n_codes, tile), F32),
            pltpu.VMEM((NZ, NC, width, tile), F32),
            pltpu.VMEM((width, n_codes), BF),
            pltpu.VMEM((n_codes, tile), F32),
            pltpu.VMEM((NZ, NC, 4, tile), F32),
            pltpu.VMEM((NZ, NC, 4, tile), F32),
            pltpu.VMEM((NPLANE, NC, 4, tile), F32),
            pltpu.VMEM((NZ, NC, 4, tile), F32),
            pltpu.VMEM((NZ, NC, 4, tile), F32),
            pltpu.VMEM((NC, NZ, tile, width), BF),
            pltpu.VMEM((NZ, tile, width), BF),
            pltpu.VMEM((NY - 1, NZ, NX * own, width), BF),
            pltpu.VMEM((NZ, NX * own, width), BF),
            pltpu.VMEM((NZ, own, width), BF),
            pltpu.VMEM((NZ, own, width), BF),
            pltpu.VMEM((NZ - 1, own, width), BF),
            pltpu.VMEM((CHUNK, width), F32),
            pltpu.VMEM((CHUNK, tile), F32),
            pltpu.VMEM((n_chunks, CHUNK, width), BF),
            pltpu.VMEM((n_chunks, CHUNK, width), BF),
            dma((NB,)), dma((NB,)),
            dma((2, half_ring, 2)), dma((2, half_ring, 2)),
            dma((2, half_ring, 2)), dma((2, half_ring, 2)),
            dma((NZ,)), dma((NZ,)),
            dma((NPLANE,)), dma((NPLANE,)),
            dma((NZ,)), dma((NZ,)),
            dma((1,)), dma((1,)),
            dma((NY,)), dma((NY,)),
            dma((1,)), dma((1,)),
            dma((NZ,)), dma((NZ,)),
            dma((n_chunks,)), dma((n_chunks,)),
        ],
        compiler_params=pltpu.CompilerParams(
            collective_id=0, has_side_effects=True, vmem_limit_bytes=60 * 1024 * 1024,
        ),
        cost_estimate=pl.CostEstimate(
            flops=10 * n_codes * n_tokens * width, bytes_accessed=4 * n_codes * width,
            transcendentals=n_codes * n_tokens,
        ),
    )(latents[0], codebook, cotangent[0])
    return quantized[None], grad


def solution(mesh):
    in_specs = (P("dp", "code", None), P("code", None), P("dp", "code", None))
    out_specs = (P("dp", "code", None), P("code", None))
    return jax.shard_map(body, mesh=mesh, in_specs=in_specs, out_specs=out_specs, check_vma=False)
```

time: 1980 us -> 91.5 us (0.05)
  blocking collectives: 1640 us -> 0 us
  waiting for transfers between devices: 260 us -> 0 us
  Pallas kernels: 0 us -> 87 us
  matrix products: 41.5 us -> 0 us
    psum x1 -> x0, blocking collectives: 549 us -> none  [body(): total = lax.psum(jnp.sum(expo, axis=1), 'code')]
    unnamed x1 -> x0, blocking collectives: 549 us -> none
    pmax x1 -> x0, blocking collectives: 544 us -> none  [body(): top = lax.pmax(jnp.max(logits, axis=1), 'code')]
    all_gather x2 -> x0, waiting for transfers between devices: 217 us -> none  [the longest x1 217 us: body(): lax.all_gather(own_lat, 'code', axis=0, tiled=True)]
    pallas_call x0 -> x1, Pallas kernels: none -> 87 us  [body(): pl.pallas_call(functools.partial(kernel, scale), out_shape=(jax.ShapeDtyp...]
    dot_general x5 -> x0, matrix products: 41.5 us -> none  [the longest x1 11.1 us: body(): jnp.dot(weights, codebook, preferred_element_type=jnp.float32)]
    psum x1 -> x0, waiting for transfers between devices: 39.7 us -> none  [body(): summed = lax.psum(local_grad.astype(jnp.bfloat16), 'dp').astype(jnp.float32)]
  transfers between devices with their start and end apart: 4 -> 0, of which waited for: 3 -> 0; matrix products, arithmetic and copies ran while one was open for 1% -> 0% of each run, Pallas kernels for 0% -> 0%
where the time goes in v1:
time: 91.5 us; the launch traced here: 91.3 us
  Pallas kernels  87 us (95%)
  local copies, waits for them, and re-layouts  3.59 us (4%)
    pallas_call x1, Pallas kernels, body(): pl.pallas_call(functools.partial(kernel, scale), out_shape=(jax.ShapeDtyp...  87 us
    unnamed x2, local copies, waits for them, and re-layouts  3.59 us

profile of v1, /device:TPU:6, one launch (start us, length us, event | category | flops | bytes accessed | tf_op | source)
XLA Modules:
  0.0 91.3 jit_solution(9553844546168823093)
XLA Ops:
  0.6 87.0 %shard_map.50 = (bf16[32,256]{1,0:T(8,128)(2,1)}, f32[1024,256]{1,0:T(8,128)}) custom-call(bf16[32,256]{1,0:T(8,128)(2,1)} %bitcast.4, bf16[1024,256]{1,0:T(8,128)(2,1)} %cb_ref.1, bf16[32,256]{1,0:T(8,128)(2,1)} %bitcast.5), custom_call_target="tpu_custom_call" | custom-call | flops 10737418240 | bytes 1048576 | tf_op jit(solution)/shard_map/pallas_call | solution.py:373
  87.7 1.3 %copy.7 = bf16[1,32,256]{2,1,0:T(8,128)(2,1)} copy(bf16[1,32,256]{2,1,0:T(8,128)(2,1)} %bitcast.3) | data formatting | bytes 32768
  89.0 2.3 %copy.8 = f32[1024,256]{1,0:T(8,128)} copy(f32[1024,256]{1,0:T(8,128)} %get-tuple-element.9) | data formatting | bytes 2097152

commit v2 on v1

v2 whole, which is shorter than its diff:
```python
import jax
import jax.numpy as jnp
from jax import lax
from jax.experimental import pallas as pl
from jax.experimental.pallas import tpu as pltpu
from jax.sharding import PartitionSpec as P

MESH = pl.DeviceIdType.MESH
NY, NZ, NX, NC = 4, 8, 2, 2
NB = NY * NX
BF, F32 = jnp.bfloat16, jnp.float32
CHUNK = 256
BY_LANE = (((1,), (1,)), ((), ()))


def kernel(
    lat_ref, cb_ref, cot_ref, q_ref, gown_ref, gin_ref,
    rows, expo, align, mixed, code_t, half, stats, pstats, smix, pmix, pairs, zparts, bparts, final, gain,
    qpart, qplane, qsend, qz, acc, slope_sum, gin,
    ag_s, ag_r, ring_s, ring_r, sib_s, sib_r, pm_s, pm_r, ps_s, ps_r, zs_s, zs_r, bp_s, bp_r, za_s, za_r, fin_s, fin_r,
    qp_s, qp_r, qz_s, qz_r, dp_s, dp_r,
):
    me = lax.axis_index("code")
    rep = lax.axis_index("dp")
    c = me % NC
    x = (me // NC) % NX
    z = (me // (NC * NX)) % NZ
    y = me // (NC * NX * NZ)
    b = y * NX + x
    own = lat_ref.shape[0]
    tile = NB * own
    n_codes, width = cb_ref.shape
    n_chunks = n_codes // CHUNK

    def dev(y_, z_, x_, c_):
        return {"code": ((y_ * NZ + z_) * NX + x_) * NC + c_}

    def send(src, dst, s_sem, r_sem, device):
        return pltpu.make_async_remote_copy(
            src_ref=src, dst_ref=dst, send_sem=s_sem, recv_sem=r_sem,
            device_id=device, device_id_type=MESH,
        )

    def block_dev(b_):
        return dev(b_ // NX, z, b_ % NX, c)

    sibling = dev(y, z, x, 1 - c)
    other_dp = {"dp": 1 - rep}

    def wait_in(ref, r_sem):
        send(ref, ref, r_sem, r_sem, sibling).wait_recv()

    barrier = pltpu.get_barrier_semaphore()
    pl.semaphore_signal(barrier, inc=1, device_id=sibling, device_id_type=MESH)
    pl.semaphore_signal(barrier, inc=1, device_id=other_dp, device_id_type=MESH)
    for d in range(1, NB):
        pl.semaphore_signal(barrier, inc=1, device_id=block_dev((b + d) % NB), device_id_type=MESH)
    for d in range(1, NZ):
        pl.semaphore_signal(barrier, inc=1, device_id=dev(y, (z + d) % NZ, x, c), device_id_type=MESH)

    own_rows = pl.ds(pl.multiple_of(b * own, own), own)
    rows[z, c, 0, own_rows, :] = lat_ref[...]
    rows[z, c, 1, own_rows, :] = cot_ref[...]

    for k in range(n_chunks):
        part = cb_ref[k * CHUNK:(k + 1) * CHUNK, :].astype(F32)
        norm = 0.5 * jnp.sum(part * part, axis=1, keepdims=True)
        half[k * CHUNK:(k + 1) * CHUNK, :] = jnp.broadcast_to(norm, (CHUNK, tile))
        code_t[:, k * CHUNK:(k + 1) * CHUNK] = jnp.transpose(part).astype(BF)

    pl.semaphore_wait(barrier, 2 + NB - 1 + NZ - 1)

    def gather_copy(d):
        block = rows.at[z, c, :, own_rows, :]
        return send(block, block, ag_s.at[d], ag_r.at[d], block_dev((b + d) % NB))

    for d in range(1, NB):
        gather_copy(d).start()

    for d in range(1, NB):
        b_ = (b + NB - d) % NB
        wait_in(rows.at[z, c, :, pl.ds(pl.multiple_of(b_ * own, own), own), :], ag_r.at[d])

    last = NZ // 2

    def zat(direction, step):
        return (z + NZ - step) % NZ if direction == 0 else (z + step) % NZ

    def ring_copy(direction, step, f):
        block = rows.at[zat(direction, step - 1), c, f]
        to = (z + 1) % NZ if direction == 0 else (z + NZ - 1) % NZ
        return send(block, block, ring_s.at[direction, step, f], ring_r.at[direction, step, f], dev(y, to, x, c))

    def sib_copy(direction, step, f):
        block = rows.at[zat(direction, step), c, f]
        return send(block, block, sib_s.at[direction, step, f], sib_r.at[direction, step, f], sibling)

    def sib_wait(direction, step, f):
        wait_in(rows.at[zat(direction, step), 1 - c, f], sib_r.at[direction, step, f])

    def arrivals(step):
        if step == 0:
            return [(0, 0), (0, 1)]
        if step == last:
            return [(0, 0), (1, 1)]
        return [(direction, f) for f in range(2) for direction in range(2)]

    def planes(step, run):
        if step == 0 or step == last:
            run((z + step) % NZ)
        else:
            @pl.loop(0, 2)
            def _(j):
                run(jnp.where(j == 0, (z + NZ - step) % NZ, (z + step) % NZ))

    def tile_forward(zp, cp):
        lat = rows[zp, cp, 0]
        cot = rows[zp, cp, 1]
        top8 = None
        for k in range(n_chunks):
            ks = slice(k * CHUNK, (k + 1) * CHUNK)
            code = cb_ref[ks, :]
            logit = lax.dot_general(code, lat, BY_LANE, preferred_element_type=F32) - half[ks, :]
            expo[zp, cp, ks, :] = logit
            align[zp, cp, ks, :] = lax.dot_general(code, cot, BY_LANE, preferred_element_type=F32)
            part = jnp.max(logit.reshape(CHUNK // 8, 8, tile), axis=0)
            top8 = part if top8 is None else jnp.maximum(top8, part)
        top = jnp.max(top8, axis=0, keepdims=True)
        total8 = jnp.zeros((8, tile), F32)
        inner8 = jnp.zeros((8, tile), F32)
        mix = jnp.zeros((width, tile), F32)
        for k in range(n_chunks):
            ks = slice(k * CHUNK, (k + 1) * CHUNK)
            e = jnp.exp(expo[zp, cp, ks, :] - top)
            expo[zp, cp, ks, :] = e
            total8 += jnp.sum(e.reshape(CHUNK // 8, 8, tile), axis=0)
            inner8 += jnp.sum((e * align[zp, cp, ks, :]).reshape(CHUNK // 8, 8, tile), axis=0)
            mix += jnp.dot(code_t[:, ks], e.astype(BF), preferred_element_type=F32)
        mixed[zp, cp] = mix
        total = jnp.sum(total8, axis=0, keepdims=True)
        inner = jnp.sum(inner8, axis=0, keepdims=True)
        stats[zp, cp] = jnp.concatenate([top, total, inner, inner], axis=0)

    def combine(part, n):
        top = part(0)[0:1, :]
        for j in range(1, n):
            top = jnp.maximum(top, part(j)[0:1, :])
        total = jnp.zeros_like(top)
        inner = jnp.zeros_like(top)
        for j in range(n):
            p = part(j)
            w = jnp.exp(p[0:1, :] - top)
            total += w * p[1:2, :]
            inner += w * p[2:3, :]
        return top, total, inner

    def pair_mix_copy(zp):
        return send(smix.at[zp], pmix.at[zp], pm_s.at[zp], pm_r.at[zp], sibling)

    def pair_stat_copy(zp):
        return send(stats.at[zp, 1 - c], pstats.at[zp], ps_s.at[zp], ps_r.at[zp], sibling)

    def pair_send(zp):
        pair_stat_copy(zp).start()
        smix[zp] = mixed[zp, 1 - c].astype(BF)
        pair_mix_copy(zp).start()

    def scatter_copy(d):
        to = (z + d) % NZ
        return send(pairs.at[to], zparts.at[z], zs_s.at[d], zs_r.at[d], dev(y, to, x, c))

    def pair_stats(zp):
        pair_stat_copy(zp).wait_recv()
        mine, other = stats[zp, c], pstats[zp]
        top = jnp.maximum(mine[0:1, :], other[0:1, :])
        w0 = jnp.exp(mine[0:1, :] - top)
        w1 = jnp.exp(other[0:1, :] - top)
        total = mine[1:2, :] * w0 + other[1:2, :] * w1
        inner = mine[2:3, :] * w0 + other[2:3, :] * w1
        pairs[zp] = jnp.concatenate([top, total, inner, inner], axis=0)

    def pair_mix(zp):
        pair_mix_copy(zp).wait_recv()
        top = pairs[zp, 0:1, :]
        w0 = jnp.exp(stats[zp, c, 0:1, :] - top)
        w1 = jnp.exp(pstats[zp, 0:1, :] - top)
        mixed[zp, c] = mixed[zp, c] * w0 + pmix[zp].astype(F32) * w1

    def pair_step(step):
        planes(step, pair_stats)
        if step == 0:
            zparts[z] = pairs[z]
        else:
            scatter_copy(step).start()
            if step < last:
                scatter_copy(NZ - step).start()

    for step in range(last + 1):
        for direction, f in arrivals(step):
            if step > 0:
                wait_in(rows.at[zat(direction, step), c, f], ring_r.at[direction, step, f])
            if step == 0:
                ring_copy(0, 1, f).start()
                ring_copy(1, 1, f).start()
            elif (direction, f) in arrivals(step + 1) and step < last:
                ring_copy(direction, step + 1, f).start()
            sib_copy(direction, step, f).start()
        if step >= 1:
            pair_step(step - 1)
            planes(step - 1, pair_mix)

        single = step == 0 or step == last
        n = 1 if single else 2

        @pl.loop(0, 2 * n)
        def _(j):
            @pl.when(j == n)
            def _():
                for direction, f in arrivals(step):
                    sib_wait(direction, step, f)
            zp = (z + step) % NZ
            if not single:
                zp = jnp.where(j % 2 == 0, (z + NZ - step) % NZ, zp)
            tile_forward(zp, (c + j // n) % 2)

        planes(step, pair_send)

    pair_step(last)

    for d in range(1, NZ):
        wait_in(zparts.at[(z + NZ - d) % NZ], zs_r.at[d])
    top, total, inner = combine(lambda j: zparts[j], NZ)
    bparts[b] = jnp.concatenate([top, total, inner, inner], axis=0)

    def block_copy(d):
        return send(bparts.at[b], bparts.at[b], bp_s.at[d], bp_r.at[d], block_dev((b + d) % NB))

    for d in range(1, NB):
        block_copy(d).start()
    planes(last, pair_mix)
    for d in range(1, NB):
        wait_in(bparts.at[(b + NB - d) % NB], bp_r.at[d])
    top, total, inner = combine(lambda j: bparts[j], NB)
    inverse = 1.0 / total
    final[c, z] = jnp.concatenate([top, inverse, inner * inverse, inner], axis=0)

    def back_copy(d):
        return send(final.at[c, z], final.at[c, z], za_s.at[d], za_r.at[d], dev(y, (z + d) % NZ, x, c))

    for d in range(1, NZ):
        back_copy(d).start()
    for d in range(1, NZ):
        wait_in(final.at[c, (z + NZ - d) % NZ], za_r.at[d])
    final_copy = send(final.at[c], final.at[c], fin_s.at[0], fin_r.at[0], sibling)
    final_copy.start()

    def set_gain(zp, cp):
        share = jnp.exp(stats[zp, cp, 0:1, :] - final[cp, zp, 0:1, :]) * final[cp, zp, 1:2, :]
        gain[zp, cp] = jnp.concatenate([share, final[cp, zp, 2:3, :], share, share], axis=0)

    @pl.loop(0, NZ)
    def _(zp):
        set_gain(zp, c)
        share = jnp.exp(pairs[zp, 0:1, :] - final[c, zp, 0:1, :]) * final[c, zp, 1:2, :]
        qpart[zp] = jnp.transpose(mixed[zp, c] * share).astype(BF)

    def quant_copy(d):
        b_ = (b + d) % NB
        part = qpart.at[:, pl.ds(pl.multiple_of(b_ * own, own), own), :]
        return send(part, qplane.at[d - 1], qp_s.at[d], qp_r.at[d], block_dev(b_))

    for d in range(1, NB):
        quant_copy(d).start()

    wait_in(final.at[1 - c], fin_r.at[0])

    @pl.loop(0, NZ)
    def _(zp):
        set_gain(zp, 1 - c)

    def dp_copy(k):
        return send(gown_ref.at[k], gin.at[k], dp_s.at[k], dp_r.at[k], other_dp)

    def grad_chunk(k):
        ks = pl.ds(pl.multiple_of(k * CHUNK, CHUNK), CHUNK)
        acc[...] = jnp.zeros_like(acc)
        slope_sum[...] = jnp.zeros_like(slope_sum)

        @pl.loop(0, NZ)
        def _(zp):
            out = acc[...]
            slopes = slope_sum[...]
            for cp in range(2):
                prob = expo[zp, cp, ks, :] * gain[zp, cp, 0:1, :]
                slope = prob * (align[zp, cp, ks, :] - gain[zp, cp, 1:2, :])
                out += jnp.dot(prob.astype(BF), rows[zp, cp, 1], preferred_element_type=F32)
                out += jnp.dot(slope.astype(BF), rows[zp, cp, 0], preferred_element_type=F32)
                slopes += slope
            acc[...] = out
            slope_sum[...] = slopes

        moved = jnp.sum(slope_sum[...], axis=1, keepdims=True) * cb_ref[ks, :].astype(F32)
        gown_ref[k] = (acc[...] - moved).astype(BF)
        dp_copy(k).start()

    def z_copy(d):
        to = (z + d) % NZ
        return send(qsend.at[to], qz.at[d - 1], qz_s.at[d], qz_r.at[d], dev(y, to, x, c))

    @pl.loop(0, n_chunks)
    def _(k):
        grad_chunk(k)

    for d in range(1, NB):
        quant_copy(d).wait_recv()
    total = qpart[:, own_rows, :].astype(F32)
    for d in range(NB - 1):
        total += qplane[d].astype(F32)
    qsend[...] = total.astype(BF)
    for d in range(1, NZ):
        z_copy(d).start()

    for d in range(1, NB):
        gather_copy(d).wait_send()
        block_copy(d).wait_send()
        quant_copy(d).wait_send()
    for step in range(last + 1):
        for direction, f in arrivals(step):
            if step > 0:
                ring_copy(direction, step, f).wait_send()
            sib_copy(direction, step, f).wait_send()
    for d in range(1, NZ):
        scatter_copy(d).wait_send()
        back_copy(d).wait_send()
    final_copy.wait_send()

    @pl.loop(0, NZ)
    def _(zp):
        pair_mix_copy(zp).wait_send()
        pair_stat_copy(zp).wait_send()

    @pl.loop(0, n_chunks)
    def _(k):
        dp_copy(k).wait()
        gin_ref[k] = gin[k]

    for d in range(1, NZ):
        z_copy(d).wait()
    quant = qsend[z].astype(F32)
    for d in range(NZ - 1):
        quant += qz[d].astype(F32)
    q_ref[...] = quant.astype(BF)


def body(latents, codebook, cotangent):
    own, width = latents.shape[1:]
    n_codes = codebook.shape[0]
    tile = NB * own
    n_chunks = n_codes // CHUNK
    n_tokens = own * lax.axis_size("code")
    scale = n_codes * lax.axis_size("code") * 1.0 / (lax.axis_size("dp") * n_tokens)
    vmem = pl.BlockSpec(memory_space=pltpu.VMEM)
    dma = pltpu.SemaphoreType.DMA
    half_ring = NZ // 2 + 1
    halves = jax.ShapeDtypeStruct((n_chunks, CHUNK, width), BF)
    quantized, here, there = pl.pallas_call(
        kernel,
        out_shape=(jax.ShapeDtypeStruct((own, width), BF), halves, halves),
        in_specs=[vmem] * 3,
        out_specs=(vmem, vmem, vmem),
        scratch_shapes=[
            pltpu.VMEM((NZ, NC, 2, tile, width), BF),
            pltpu.VMEM((NZ, NC, n_codes, tile), F32),
            pltpu.VMEM((NZ, NC, n_codes, tile), F32),
            pltpu.VMEM((NZ, NC, width, tile), F32),
            pltpu.VMEM((width, n_codes), BF),
            pltpu.VMEM((n_codes, tile), F32),
            pltpu.VMEM((NZ, NC, 4, tile), F32),
            pltpu.VMEM((NZ, 4, tile), F32),
            pltpu.VMEM((NZ, width, tile), BF),
            pltpu.VMEM((NZ, width, tile), BF),
            pltpu.VMEM((NZ, 4, tile), F32),
            pltpu.VMEM((NZ, 4, tile), F32),
            pltpu.VMEM((NB, 4, tile), F32),
            pltpu.VMEM((NC, NZ, 4, tile), F32),
            pltpu.VMEM((NZ, NC, 4, tile), F32),
            pltpu.VMEM((NZ, tile, width), BF),
            pltpu.VMEM((NB - 1, NZ, own, width), BF),
            pltpu.VMEM((NZ, own, width), BF),
            pltpu.VMEM((NZ - 1, own, width), BF),
            pltpu.VMEM((CHUNK, width), F32),
            pltpu.VMEM((CHUNK, tile), F32),
            pltpu.VMEM((n_chunks, CHUNK, width), BF),
            dma((NB,)), dma((NB,)),
            dma((2, half_ring, 2)), dma((2, half_ring, 2)),
            dma((2, half_ring, 2)), dma((2, half_ring, 2)),
            dma((NZ,)), dma((NZ,)),
            dma((NZ,)), dma((NZ,)),
            dma((NZ,)), dma((NZ,)),
            dma((NB,)), dma((NB,)),
            dma((NZ,)), dma((NZ,)),
            dma((1,)), dma((1,)),
            dma((NB,)), dma((NB,)),
            dma((NZ,)), dma((NZ,)),
            dma((n_chunks,)), dma((n_chunks,)),
        ],
        compiler_params=pltpu.CompilerParams(
            collective_id=0, has_side_effects=True, vmem_limit_bytes=60 * 1024 * 1024,
        ),
        cost_estimate=pl.CostEstimate(
            flops=10 * n_codes * n_tokens * width, bytes_accessed=4 * n_codes * width,
            transcendentals=n_codes * n_tokens,
        ),
    )(latents[0], codebook, cotangent[0])
    grad = (here.astype(F32) + there.astype(F32)) * scale
    return quantized[None], grad.reshape(n_codes, width)


def solution(mesh):
    in_specs = (P("dp", "code", None), P("code", None), P("dp", "code", None))
    out_specs = (P("dp", "code", None), P("code", None))
    return jax.shard_map(body, mesh=mesh, in_specs=in_specs, out_specs=out_specs, check_vma=False)
```

time: 91.5 us -> 86.4 us (0.944)
  Pallas kernels: 87 us -> 81.9 us
  local copies, waits for them, and re-layouts: 3.59 us -> 0.61 us
  other arithmetic: 0 us -> 2.32 us
    pallas_call x1, Pallas kernels: 87 us -> 81.9 us  [body(): pl.pallas_call(kernel, out_shape=(jax.ShapeDtypeStruct((own, width), BF),...]
    unnamed x2 -> x3, local copies, waits for them, and re-layouts: 3.59 us -> 0.61 us
    mul x0 -> x1, other arithmetic: none -> 2.32 us  [body(): grad = (here.astype(F32) + there.astype(F32)) * scale]
where the time goes in v2:
time: 86.4 us; the launch traced here: 85.4 us
  Pallas kernels  81.9 us (95%)
  other arithmetic  2.32 us (3%)
    pallas_call x1, Pallas kernels, body(): pl.pallas_call(kernel, out_shape=(jax.ShapeDtypeStruct((own, width), BF),...  81.9 us
    mul x1, other arithmetic, body(): grad = (here.astype(F32) + there.astype(F32)) * scale  2.32 us

profile of v2, /device:TPU:6, one launch (start us, length us, event | category | flops | bytes accessed | tf_op | source)
XLA Modules:
  0.0 85.4 jit_solution(15268990966985665106)
XLA Ops:
  0.6 81.9 %shard_map.50 = (bf16[32,256]{1,0:T(8,128)(2,1)}, bf16[4,256,256]{2,1,0:T(8,128)(2,1)}, bf16[4,256,256]{2,1,0:T(8,128)(2,1)}) custom-call(bf16[32,256]{1,0:T(8,128)(2,1)} %bitcast.6, bf16[1024,256]{1,0:T(8,128)(2,1)} %cb_ref.1, bf16[32,256]{1,0:T(8,128)(2,1)} %bitcast.7), custom_call_target="tpu_custom_call" | custom-call | flops 10737418240 | bytes 1048576 | tf_op jit(solution)/shard_map/pallas_call | solution.py:366
  82.5 0.0 copy-start
  82.5 2.3 %add_multiply_fusion = f32[4,256,256]{2,1,0:T(8,128)} fusion(bf16[4,256,256]{2,1,0:T(8,128)(2,1)} %get-tuple-element.7, bf16[4,256,256]{2,1,0:T(8,128)(2,1)} %get-tuple-element.6), kind=kLoop, calls=%fused_computation | loop fusion | flops 1048576 | bytes 2097152 | tf_op jit(solution)/shard_map/mul | solution.py:415
  84.8 0.0 copy-done
  84.8 0.6 copy.6
Async XLA Ops:
  82.5 2.3 %copy-start = (bf16[32,256]{1,0:T(8,128)(2,1)S(1)}, bf16[32,256]{1,0:T(8,128)(2,1)}, u32[]{:S(2)}) copy-start(bf16[32,256]{1,0:T(8,128)(2,1)} %get-tuple-element.5) | copy-start | bytes 49156

commit v3 on v2

--- a/solution.py
+++ b/solution.py
@@ -16,8 +16,8 @@
 def kernel(
     lat_ref, cb_ref, cot_ref, q_ref, gown_ref, gin_ref,
     rows, expo, align, mixed, code_t, half, stats, pstats, smix, pmix, pairs, zparts, bparts, final, gain,
-    qpart, qplane, qsend, qz, acc, slope_sum, gin,
-    ag_s, ag_r, ring_s, ring_r, sib_s, sib_r, pm_s, pm_r, ps_s, ps_r, zs_s, zs_r, bp_s, bp_r, za_s, za_r, fin_s, fin_r,
+    qpart, qplane, qsend, qz, gin,
+    ag_s, ag_r, zx_s, zx_r, col_s, col_r, ring_s, ring_r, sib_s, sib_r, pm_s, pm_r, ps_s, ps_r, zs_s, zs_r, bp_s, bp_r, za_s, za_r, fin_s, fin_r,
     qp_s, qp_r, qz_s, qz_r, dp_s, dp_r,
 ):
     me = lax.axis_index("code")
@@ -50,6 +50,9 @@
     def wait_in(ref, r_sem):
         send(ref, ref, r_sem, r_sem, sibling).wait_recv()
 
+    def wait_out(ref, s_sem):
+        send(ref, ref, s_sem, s_sem, sibling).wait_send()
+
     barrier = pltpu.get_barrier_semaphore()
     pl.semaphore_signal(barrier, inc=1, device_id=sibling, device_id_type=MESH)
     pl.semaphore_signal(barrier, inc=1, device_id=other_dp, device_id_type=MESH)
@@ -66,20 +69,50 @@
         part = cb_ref[k * CHUNK:(k + 1) * CHUNK, :].astype(F32)
         norm = 0.5 * jnp.sum(part * part, axis=1, keepdims=True)
         half[k * CHUNK:(k + 1) * CHUNK, :] = jnp.broadcast_to(norm, (CHUNK, tile))
+
+    pl.semaphore_wait(barrier, 2 + NB - 1 + NZ - 1)
+
+    def gather_copy(d, f):
+        block = rows.at[z, c, f, own_rows, :]
+        return send(block, block, ag_s.at[d, f], ag_r.at[d, f], block_dev((b + d) % NB))
+
+    def gather_wait(f):
+        for d in range(1, NB):
+            b_ = (b + NB - d) % NB
+            wait_in(rows.at[z, c, f, pl.ds(pl.multiple_of(b_ * own, own), own), :], ag_r.at[d, f])
+
+    def spread_copy(d):
+        block = rows.at[z, c, :, own_rows, :]
+        return send(block, block, zx_s.at[d], zx_r.at[d], dev(y, (z + d) % NZ, x, c))
+
+    def column_send(zp):
+        block = rows.at[zp, c, :, own_rows, :]
+        for d in range(1, NB):
+            send(block, block, col_s.at[zp], col_r.at[zp], block_dev((b + d) % NB)).start()
+
+    def column_wait(zp):
+        wait_in(rows.at[zp, c, :, 0:(NB - 1) * own, :], col_r.at[zp])
+
+    @pl.when(c == 0)
+    def _():
+        for d in range(1, NB):
+            gather_copy(d, 0).start()
+
+    @pl.when(c == 1)
+    def _():
+        for d in range(1, NZ):
+            spread_copy(d).start()
+
+    for k in range(n_chunks):
+        part = cb_ref[k * CHUNK:(k + 1) * CHUNK, :].astype(F32)
         code_t[:, k * CHUNK:(k + 1) * CHUNK] = jnp.transpose(part).astype(BF)
 
-    pl.semaphore_wait(barrier, 2 + NB - 1 + NZ - 1)
-
-    def gather_copy(d):
-        block = rows.at[z, c, :, own_rows, :]
-        return send(block, block, ag_s.at[d], ag_r.at[d], block_dev((b + d) % NB))
-
-    for d in range(1, NB):
-        gather_copy(d).start()
-
-    for d in range(1, NB):
-        b_ = (b + NB - d) % NB
-        wait_in(rows.at[z, c, :, pl.ds(pl.multiple_of(b_ * own, own), own), :], ag_r.at[d])
+    @pl.when(c == 0)
+    def _():
+        for d in range(1, NB):
+            gather_copy(d, 0).wait_send()
+        for d in range(1, NB):
+            gather_copy(d, 1).start()
 
     last = NZ // 2
 
@@ -91,25 +124,14 @@
         to = (z + 1) % NZ if direction == 0 else (z + NZ - 1) % NZ
         return send(block, block, ring_s.at[direction, step, f], ring_r.at[direction, step, f], dev(y, to, x, c))
 
-    def sib_copy(direction, step, f):
-        block = rows.at[zat(direction, step), c, f]
-        return send(block, block, sib_s.at[direction, step, f], sib_r.at[direction, step, f], sibling)
-
-    def sib_wait(direction, step, f):
-        wait_in(rows.at[zat(direction, step), 1 - c, f], sib_r.at[direction, step, f])
-
-    def arrivals(step):
-        if step == 0:
-            return [(0, 0), (0, 1)]
-        if step == last:
-            return [(0, 0), (1, 1)]
-        return [(direction, f) for f in range(2) for direction in range(2)]
+    def sib_copy(zp):
+        return send(rows.at[zp, c], rows.at[zp, c], sib_s.at[zp], sib_r.at[zp], sibling)
 
     def planes(step, run):
-        if step == 0 or step == last:
+        if isinstance(step, int) and step in (0, last):
             run((z + step) % NZ)
         else:
-            @pl.loop(0, 2)
+            @pl.loop(0, jnp.minimum(step + 1, 2))
             def _(j):
                 run(jnp.where(j == 0, (z + NZ - step) % NZ, (z + step) % NZ))
 
@@ -188,44 +210,105 @@
 
     def pair_step(step):
         planes(step, pair_stats)
-        if step == 0:
+
+        @pl.when(step == 0)
+        def _():
             zparts[z] = pairs[z]
-        else:
+
+        @pl.when(step > 0)
+        def _():
             scatter_copy(step).start()
-            if step < last:
-                scatter_copy(NZ - step).start()
-
-    for step in range(last + 1):
-        for direction, f in arrivals(step):
-            if step > 0:
-                wait_in(rows.at[zat(direction, step), c, f], ring_r.at[direction, step, f])
-            if step == 0:
-                ring_copy(0, 1, f).start()
-                ring_copy(1, 1, f).start()
-            elif (direction, f) in arrivals(step + 1) and step < last:
-                ring_copy(direction, step + 1, f).start()
-            sib_copy(direction, step, f).start()
-        if step >= 1:
-            pair_step(step - 1)
-            planes(step - 1, pair_mix)
-
-        single = step == 0 or step == last
-        n = 1 if single else 2
-
-        @pl.loop(0, 2 * n)
-        def _(j):
-            @pl.when(j == n)
+
+        @pl.when((step > 0) & (step < last))
+        def _():
+            scatter_copy(NZ - step).start()
+
+    def own_tiles(step):
+        planes(step, lambda zp: tile_forward(zp, c))
+
+    def sib_tiles(step):
+        def run(zp):
+            wait_in(rows.at[zp, 1 - c], sib_r.at[zp])
+            tile_forward(zp, 1 - c)
+            pair_send(zp)
+
+        planes(step, run)
+
+    def ring_wait(direction, step, f):
+        wait_in(rows.at[zat(direction, step), c, f], ring_r.at[direction, step, f])
+
+    @pl.when(c == 0)
+    def _():
+        for f in range(2):
+            gather_wait(f)
+            for direction in range(2):
+                ring_copy(direction, 1, f).start()
+
+    @pl.when(c == 1)
+    def _():
+        for d in range(1, NZ):
+            block = rows.at[(z + NZ - d) % NZ, c, :, own_rows, :]
+            wait_in(block, zx_r.at[d])
+        column_send(z)
+        for direction in range(2):
+            column_send(zat(direction, 1))
+        column_wait(z)
+
+    sib_copy(z).start()
+    own_tiles(0)
+
+    @pl.loop(1, last)
+    def _(s):
+        for f in range(2):
+            @pl.when(c == 0)
             def _():
-                for direction, f in arrivals(step):
-                    sib_wait(direction, step, f)
-            zp = (z + step) % NZ
-            if not single:
-                zp = jnp.where(j % 2 == 0, (z + NZ - step) % NZ, zp)
-            tile_forward(zp, (c + j // n) % 2)
-
-        planes(step, pair_send)
-
-    pair_step(last)
+                for direction in range(2):
+                    ring_wait(direction, s, f)
+                    if direction == f:
+                        ring_copy(direction, s + 1, f).start()
+                    else:
+                        @pl.when(s + 1 < last)
+                        def _():
+                            ring_copy(direction, s + 1, f).start()
+
+            @pl.when(c == 1)
+            def _():
+                column_wait(zat(f, s))
+                if f == 0:
+                    column_send(zat(0, s + 1))
+                else:
+                    @pl.when(s + 1 < last)
+                    def _():
+                        column_send(zat(1, s + 1))
+
+            if f == 0:
+                sib_tiles(s - 1)
+            else:
+                planes(s, lambda zp: sib_copy(zp).start())
+                own_tiles(s)
+                pair_step(s - 1)
+                planes(s - 1, pair_mix)
+
+    sib_tiles(last - 1)
+
+    @pl.when(c == 0)
+    def _():
+        ring_wait(0, last, 0)
+        ring_wait(1, last, 1)
+
+    @pl.when(c == 1)
+    def _():
+        column_wait((z + last) % NZ)
+
+    sib_copy((z + last) % NZ).start()
+    own_tiles(last)
+    pair_step(last - 1)
+    planes(last - 1, pair_mix)
+    wait_in(rows.at[(z + last) % NZ, 1 - c], sib_r.at[(z + last) % NZ])
+    tile_forward((z + last) % NZ, 1 - c)
+    pair_send((z + last) % NZ)
+    planes(last, pair_stats)
+    scatter_copy(last).start()
 
     for d in range(1, NZ):
         wait_in(zparts.at[(z + NZ - d) % NZ], zs_r.at[d])
@@ -283,24 +366,17 @@
 
     def grad_chunk(k):
         ks = pl.ds(pl.multiple_of(k * CHUNK, CHUNK), CHUNK)
-        acc[...] = jnp.zeros_like(acc)
-        slope_sum[...] = jnp.zeros_like(slope_sum)
-
-        @pl.loop(0, NZ)
-        def _(zp):
-            out = acc[...]
-            slopes = slope_sum[...]
+        out = jnp.zeros((CHUNK, width), F32)
+        slopes = jnp.zeros((CHUNK, tile), F32)
+        for zp in range(NZ):
             for cp in range(2):
                 prob = expo[zp, cp, ks, :] * gain[zp, cp, 0:1, :]
                 slope = prob * (align[zp, cp, ks, :] - gain[zp, cp, 1:2, :])
                 out += jnp.dot(prob.astype(BF), rows[zp, cp, 1], preferred_element_type=F32)
                 out += jnp.dot(slope.astype(BF), rows[zp, cp, 0], preferred_element_type=F32)
                 slopes += slope
-            acc[...] = out
-            slope_sum[...] = slopes
-
-        moved = jnp.sum(slope_sum[...], axis=1, keepdims=True) * cb_ref[ks, :].astype(F32)
-        gown_ref[k] = (acc[...] - moved).astype(BF)
+        moved = jnp.sum(slopes, axis=1, keepdims=True) * cb_ref[ks, :].astype(F32)
+        gown_ref[k] = (out - moved).astype(BF)
         dp_copy(k).start()
 
     def z_copy(d):
@@ -321,14 +397,29 @@
         z_copy(d).start()
 
     for d in range(1, NB):
-        gather_copy(d).wait_send()
         block_copy(d).wait_send()
         quant_copy(d).wait_send()
-    for step in range(last + 1):
-        for direction, f in arrivals(step):
-            if step > 0:
-                ring_copy(direction, step, f).wait_send()
-            sib_copy(direction, step, f).wait_send()
+
+    @pl.when(c == 0)
+    def _():
+        for d in range(1, NB):
+            gather_copy(d, 1).wait_send()
+        for f in range(2):
+            @pl.loop(1, last)
+            def _(s):
+                for direction in range(2):
+                    ring_copy(direction, s, f).wait_send()
+            ring_copy(f, last, f).wait_send()
+
+    @pl.when(c == 1)
+    def _():
+        for d in range(1, NZ):
+            spread_copy(d).wait_send()
+
+        @pl.loop(0, NZ)
+        def _(zp):
+            wait_out(rows.at[zp, c, :, 0:(NB - 1) * own, :], col_s.at[zp])
+
     for d in range(1, NZ):
         scatter_copy(d).wait_send()
         back_copy(d).wait_send()
@@ -336,6 +427,7 @@
 
     @pl.loop(0, NZ)
     def _(zp):
+        sib_copy(zp).wait_send()
         pair_mix_copy(zp).wait_send()
         pair_stat_copy(zp).wait_send()
 
@@ -388,12 +480,12 @@
             pltpu.VMEM((NB - 1, NZ, own, width), BF),
             pltpu.VMEM((NZ, own, width), BF),
             pltpu.VMEM((NZ - 1, own, width), BF),
-            pltpu.VMEM((CHUNK, width), F32),
-            pltpu.VMEM((CHUNK, tile), F32),
             pltpu.VMEM((n_chunks, CHUNK, width), BF),
-            dma((NB,)), dma((NB,)),
+            dma((NB, 2)), dma((NB, 2)),
+            dma((NZ,)), dma((NZ,)),
+            dma((NZ,)), dma((NZ,)),
             dma((2, half_ring, 2)), dma((2, half_ring, 2)),
-            dma((2, half_ring, 2)), dma((2, half_ring, 2)),
+            dma((NZ,)), dma((NZ,)),
             dma((NZ,)), dma((NZ,)),
             dma((NZ,)), dma((NZ,)),
             dma((NZ,)), dma((NZ,)),

time: 86.4 us -> 82.8 us (0.958)
  Pallas kernels: 81.9 us -> 78.4 us
    pallas_call x1, Pallas kernels: 81.9 us -> 78.4 us  [body(): pl.pallas_call(kernel, out_shape=(jax.ShapeDtypeStruct((own, width), BF),...]
where the time goes in v3:
time: 82.8 us; the launch traced here: 82 us
  Pallas kernels  78.4 us (95%)
  other arithmetic  2.32 us (3%)
    pallas_call x1, Pallas kernels, body(): pl.pallas_call(kernel, out_shape=(jax.ShapeDtypeStruct((own, width), BF),...  78.4 us
    mul x1, other arithmetic, body(): grad = (here.astype(F32) + there.astype(F32)) * scale  2.32 us

profile of v3, /device:TPU:6, one launch (start us, length us, event | category | flops | bytes accessed | tf_op | source)
XLA Modules:
  0.0 82.0 jit_solution(10923463216616995482)
XLA Ops:
  0.6 78.4 %shard_map.50 = (bf16[32,256]{1,0:T(8,128)(2,1)}, bf16[4,256,256]{2,1,0:T(8,128)(2,1)}, bf16[4,256,256]{2,1,0:T(8,128)(2,1)}) custom-call(bf16[32,256]{1,0:T(8,128)(2,1)} %bitcast.6, bf16[1024,256]{1,0:T(8,128)(2,1)} %cb_ref.1, bf16[32,256]{1,0:T(8,128)(2,1)} %bitcast.7), custom_call_target="tpu_custom_call" | custom-call | flops 10737418240 | bytes 1048576 | tf_op jit(solution)/shard_map/pallas_call | solution.py:458
  79.0 0.0 copy-start
  79.0 2.3 %add_multiply_fusion = f32[4,256,256]{2,1,0:T(8,128)} fusion(bf16[4,256,256]{2,1,0:T(8,128)(2,1)} %get-tuple-element.7, bf16[4,256,256]{2,1,0:T(8,128)(2,1)} %get-tuple-element.6), kind=kLoop, calls=%fused_computation | loop fusion | flops 1048576 | bytes 2097152 | tf_op jit(solution)/shard_map/mul | solution.py:507
  81.4 0.0 copy-done
  81.4 0.6 copy.6
Async XLA Ops:
  79.0 2.3 %copy-start = (bf16[32,256]{1,0:T(8,128)(2,1)S(1)}, bf16[32,256]{1,0:T(8,128)(2,1)}, u32[]{:S(2)}) copy-start(bf16[32,256]{1,0:T(8,128)(2,1)} %get-tuple-element.5) | copy-start | bytes 49156
